TPU v7x, 256 devices: a whole 4x4x8 slice. The times are simulated.
256 devices in a mesh: tm: 32 (over y, z_lo, core), head: 8 (over z_hi, x).
Axes of the slice: x: 4, y: 4, z: 8 (z_hi: 2, z_lo: 4; z = z_hi * 4 + z_lo), core: 2. Of those that a mesh axis runs over, the one named last changes fastest.
Arguments:
- latents: bfloat16 [16384, 3072], P(('tm', 'head')), may hold values from -6 to 6
- cotangent: bfloat16 [16384, 3072], P(('tm', 'head')), may hold values from -6 to 6
- norm_gain: float32 [3072], replicated, may hold values from 0.1 to 1.9
- w_qkv: bfloat16 [3072, 3, 3072], P(None, None, 'head'), may hold values from -0.114763592 to 0.114763592
- w_out: bfloat16 [3072, 3072], P('head'), may hold values from -0.109375 to 0.109375
Outputs:
- input_grad: bfloat16 [16384, 3072], P(('tm', 'head'))
All inputs are finite; a program needn't handle non-finite values.
Results may differ from a plain program's by a relative error of at most 0.012.
Values may be sent and summed in bfloat16 or wider, within the bound.
A program may use at most 128 MiB of HBM per device.

v0:
```python
import jax
import jax.numpy as jnp
from jax import lax
from jax.sharding import PartitionSpec as P

HEAD_DIM = 128
EPSILON = 1e-06


def from_behind(block, axis, distance):
    devices = range(lax.axis_size(axis))
    route = [(i - distance, i) for i in devices if i - distance in devices]
    return lax.ppermute(block, axis, route)


def scores_of(queries, keys):
    return jnp.einsum(
        "phe,khe->hpk", queries, keys, preferred_element_type=jnp.float32
    ) * HEAD_DIM ** (-0.5)


def shards(latents, cotangent, norm_gain, w_qkv, w_out):
    feature_count = latents.shape[1]
    local_width = w_qkv.shape[2]
    heads_here = local_width // HEAD_DIM
    scale = HEAD_DIM ** (-0.5)
    latent_f = latents.astype(jnp.float32)
    inv_rms = lax.rsqrt(jnp.mean(latent_f * latent_f, axis=-1, keepdims=True) + EPSILON)
    normed = latent_f * inv_rms
    hidden = (normed * norm_gain).astype(jnp.bfloat16)
    flat_w = w_qkv.reshape(feature_count, 3 * local_width)
    projected = jnp.dot(
        lax.all_gather(hidden, "head", axis=0, tiled=True),
        flat_w,
        preferred_element_type=jnp.float32,
    ).astype(jnp.bfloat16)
    frame_len = projected.shape[0]
    shape3 = (frame_len, heads_here, HEAD_DIM)
    queries = projected[:, :local_width].reshape(shape3)
    keys_own = projected[:, local_width : 2 * local_width].reshape(shape3)
    values_own = projected[:, 2 * local_width :].reshape(shape3)
    keys_prev, values_prev = from_behind((keys_own, values_own), "tm", 1)
    has_prev = (lax.axis_index("tm") > 0).astype(jnp.float32)
    grad_attn = (
        lax.dot_general(
            lax.all_gather(cotangent, "head", axis=0, tiled=True),
            w_out,
            (((1,), (1,)), ((), ())),
            preferred_element_type=jnp.float32,
        )
        .astype(jnp.bfloat16)
        .reshape(shape3)
    )
    own_s = scores_of(queries, keys_own)
    prev_s = scores_of(queries, keys_prev)
    row_top = jnp.maximum(
        jnp.max(own_s, axis=-1), jnp.where(has_prev > 0.5, jnp.max(prev_s, axis=-1), -1e30)
    )
    own_e = jnp.exp(own_s - row_top[..., None])
    prev_e = jnp.exp(prev_s - row_top[..., None]) * has_prev
    row_total = jnp.sum(own_e, axis=-1) + jnp.sum(prev_e, axis=-1)
    own_p = own_e / row_total[..., None]
    prev_p = prev_e / row_total[..., None]
    own_dp = jnp.einsum("phe,khe->hpk", grad_attn, values_own, preferred_element_type=jnp.float32)
    prev_dp = jnp.einsum("phe,khe->hpk", grad_attn, values_prev, preferred_element_type=jnp.float32)
    row_delta = jnp.sum(own_p * own_dp, axis=-1) + jnp.sum(prev_p * prev_dp, axis=-1)
    own_ds = (own_p * (own_dp - row_delta[..., None]) * scale).astype(jnp.bfloat16)
    prev_ds = (prev_p * (prev_dp - row_delta[..., None]) * scale).astype(jnp.bfloat16)
    grad_query = (
        jnp.einsum("hpk,khe->phe", own_ds, keys_own, preferred_element_type=jnp.float32)
        + jnp.einsum("hpk,khe->phe", prev_ds, keys_prev, preferred_element_type=jnp.float32)
    ).astype(jnp.bfloat16)
    key_own_g = jnp.einsum("hpk,phe->khe", own_ds, queries, preferred_element_type=jnp.float32)
    value_own_g = jnp.einsum(
        "hpk,phe->khe", own_p.astype(jnp.bfloat16), grad_attn, preferred_element_type=jnp.float32
    )
    key_back_g = jnp.einsum(
        "hpk,phe->khe", prev_ds, queries, preferred_element_type=jnp.float32
    ).astype(jnp.bfloat16)
    value_back_g = jnp.einsum(
        "hpk,phe->khe", prev_p.astype(jnp.bfloat16), grad_attn, preferred_element_type=jnp.float32
    ).astype(jnp.bfloat16)
    key_next, value_next = from_behind((key_back_g, value_back_g), "tm", -1)
    grad_key = (key_own_g + key_next.astype(jnp.float32)).astype(jnp.bfloat16)
    grad_value = (value_own_g + value_next.astype(jnp.float32)).astype(jnp.bfloat16)
    grad_qkv = jnp.concatenate(
        [
            grad_query.reshape(frame_len, local_width),
            grad_key.reshape(frame_len, local_width),
            grad_value.reshape(frame_len, local_width),
        ],
        axis=1,
    )
    grad_hidden = lax.psum_scatter(
        lax.dot_general(
            grad_qkv, flat_w, (((1,), (1,)), ((), ())), preferred_element_type=jnp.float32
        ).astype(jnp.bfloat16),
        "head",
        scatter_dimension=0,
        tiled=True,
    ).astype(jnp.float32)
    grad_normed = grad_hidden * norm_gain
    inner = jnp.mean(grad_normed * normed, axis=-1, keepdims=True)
    result = cotangent.astype(jnp.float32) + inv_rms * (grad_normed - normed * inner)
    return result.astype(jnp.bfloat16)


def solution(mesh):
    return jax.shard_map(
        shards,
        mesh=mesh,
        in_specs=(
            P(("tm", "head"), None),
            P(("tm", "head"), None),
            P(),
            P(None, None, "head"),
            P("head", None),
        ),
        out_specs=P(("tm", "head"), None),
        check_vma=False,
    )
```

profile of v0, /device:TPU:8, one launch (start us, length us, event | category | flops | bytes accessed | tf_op | source)
XLA Modules:
  0.0 347.7 jit_solution(16157256869247840403)
XLA Ops:
  6.5 0.0 copy-start
  6.5 0.0 all-gather.3.cloned.1.call-start
  6.5 1.3 fusion.33
  7.9 1.9 fusion.27
  9.8 0.0 all-gather.3.cloned.1.call-update
  9.8 0.0 all-gather.5.cloned.1.call-start
  9.9 0.7 all-gather.5.cloned.1.call-update
  10.6 0.0 reduce-scatter.2.cloned.1.call-start
  10.6 10.3 %copy.24 = bf16[3072,3,384]{0,2,1:T(8,128)(2,1)} copy(bf16[3072,3,384]{2,0,1:T(8,128)(2,1)} %param.8) | data formatting | bytes 14155776 | tf_op args[3]
  20.9 83.8 %all-gather.3.cloned.1.call-done = bf16[512,3072]{1,0:T(8,128)(2,1)} async-done(((bf16[64,3072]{1,0:T(8,128)(2,1)}), bf16[512,3072]{1,0:T(8,128)(2,1)}) %all-gather.3.cloned.1.call-update) | async-done | bytes 3145744 | tf_op jit(solution)/shard_map/all_gather | solution.py:33
  104.7 8.2 %convolution_convert_fusion.1 = bf16[512,1152]{1,0:T(8,128)(2,1)S(1)} fusion(bf16[512,3072]{1,0:T(8,128)(2,1)} %all-gather.3.cloned.1.call-done, bf16[3072,1152]{0,1:T(8,128)(2,1)} %bitcast.47), kind=kOutput, calls=%fused_computation.7 | convolution fusion | flops 3624468480 | bytes 11403264 | tf_op jit(solution)/shard_map/dot_general | solution.py:32
  112.9 0.9 fusion.39
  113.8 0.2 copy.31
  114.0 0.9 copy.34
  114.9 1.2 copy.25
  116.1 0.9 copy.29
  117.0 1.9 collective-permute-start
  118.9 2.6 collective-permute-start.1
  121.6 73.9 %all-gather.5.cloned.1.call-done = bf16[512,3072]{1,0:T(8,128)(2,1)} async-done(((bf16[64,3072]{1,0:T(8,128)(2,1)}), bf16[512,3072]{1,0:T(8,128)(2,1)}) %all-gather.5.cloned.1.call-update) | async-done | bytes 3145744 | tf_op jit(solution)/shard_map/all_gather | solution.py:46
  195.5 0.0 copy-done
  195.5 3.3 convolution_convert_fusion.3
  198.8 0.0 copy-start.4
  198.8 2.3 fusion.40
  201.2 0.0 copy-done.4
  201.2 0.2 copy.26
  201.4 0.6 multiply_reduce_fusion.3
  202.0 0.0 collective-permute-done
  202.0 1.6 multiply_reduce_fusion.2
  203.6 0.0 copy-start.5
  203.6 1.1 fusion.3
  204.8 0.0 copy-done.5
  204.8 0.0 copy-start.1
  204.8 0.9 fusion.16
  205.7 2.1 collective-permute-start.3
  207.8 0.0 collective-permute-done.1
  207.8 0.0 copy-done.1
  207.9 2.7 multiply_reduce_fusion
  210.6 2.0 multiply_convert_fusion
  212.6 0.4 fusion.41
  213.0 0.6 fusion.15
  213.6 1.9 collective-permute-start.2
  215.5 0.0 slice-start
  215.5 1.6 fusion.14
  217.1 0.0 slice-start.1
  217.1 0.0 collective-permute-done.3
  217.1 0.9 add_convert_fusion
  218.0 2.8 collective-permute-done.2
  220.8 0.6 add_convert_fusion.1
  221.4 0.0 slice-done
  221.5 0.0 slice-done.1
  221.5 5.8 %convolution_convert_fusion = bf16[512,3072]{1,0:T(8,128)(2,1)} fusion(bf16[3072,1152]{0,1:T(8,128)(2,1)S(1)} %bitcast.50, bf16[512,384]{0,1:T(8,128)(2,1)S(1)} %bitcast.62, bf16[512,384]{0,1:T(8,128)(2,1)S(1)} %bitcast.57, bf16[512,384]{0,1:T(8,128)(2,1)S(1)} %bitcast.56), kind=kOutput, calls=%fused_computation | convolution fusion | flops 3628990464 | bytes 11403264 | tf_op jit(solution)/shard_map/dot_general | solution.py:95
  227.3 0.0 copy-start.2
  227.3 0.0 copy-start.6
  227.3 0.0 copy-start.3
  227.3 0.0 reduce-scatter.2.cloned.1.call-update
  227.3 110.5 %reduce-scatter.2.cloned.1.call-done = bf16[64,3072]{1,0:T(8,128)(2,1)} async-done(((bf16[512,3072]{1,0:T(8,128)(2,1)}), bf16[64,3072]{1,0:T(8,128)(2,1)}) %reduce-scatter.2.cloned.1.call-update) | async-done | bytes 393232 | tf_op jit(solution)/shard_map/reduce_scatter | solution.py:94
  337.8 0.0 copy-done.2
  337.8 0.0 copy-done.6
  337.8 1.3 fusion.28
  339.1 0.0 copy-done.3
  339.1 2.0 fusion.32
  (6 shorter events, 0.0 us)
Async XLA Ops:
  6.5 189.0 %copy-start = (bf16[384,3072]{1,0:T(8,128)(2,1)S(1)}, bf16[384,3072]{1,0:T(8,128)(2,1)}, u32[]{:S(2)}) copy-start(bf16[384,3072]{1,0:T(8,128)(2,1)} %param.9) | copy-start | bytes 7077892
  6.5 98.1 %all-gather.3.cloned.1.call-start = ((), (), s32[]{:S(2)}) async-start(), calls=%async_computation.1 | async-start | bytes 3538944 | tf_op jit(solution)/shard_map/all_gather | solution.py:33
  9.8 185.7 %all-gather.5.cloned.1.call-start = ((), (), s32[]{:S(2)}) async-start(), calls=%async_computation.2 | async-start | bytes 3538944 | tf_op jit(solution)/shard_map/all_gather | solution.py:46
  10.6 327.2 %reduce-scatter.2.cloned.1.call-start = ((), (), s32[]{:S(2)}) async-start(), calls=%async_computation.3 | async-start | bytes 3538944 | tf_op jit(solution)/shard_map/reduce_scatter | solution.py:94
  117.0 85.0 %collective-permute-start = (bf16[512,3,128]{2,0,1:T(8,128)(2,1)}, bf16[512,3,128]{2,0,1:T(8,128)(2,1)}, u32[]{:S(2)}, u32[]{:S(2)}) collective-permute-start(bf16[512,3,128]{2,0,1:T(8,128)(2,1)} %copy.29), channel_id=1, source_target_pairs={{0,8},{8,16},{16,24},{24,32},{32,40},{40,48},{48,56},{56,64},{64,7... | collective-permute-start | bytes 1179656 | tf_op jit(solution)/shard_map/ppermute | solution.py:13
  118.9 88.9 %collective-permute-start.1 = (bf16[512,3,128]{2,0,1:T(8,128)(2,1)}, bf16[512,3,128]{2,0,1:T(8,128)(2,1)}, u32[]{:S(2)}, u32[]{:S(2)}) collective-permute-start(bf16[512,3,128]{2,0,1:T(8,128)(2,1)} %copy.34), channel_id=1, source_target_pairs={{0,8},{8,16},{16,24},{24,32},{32,40},{40,48},{48,56},{56,64},{64,7... | collective-permute-start | bytes 1179656 | tf_op jit(solution)/shard_map/ppermute | solution.py:13
  198.8 2.4 copy-start.4
  203.6 1.2 copy-start.5
  204.8 3.1 copy-start.1
  205.7 11.4 %collective-permute-start.3 = (bf16[512,3,128]{0,2,1:T(8,128)(2,1)S(1)}, bf16[512,3,128]{0,2,1:T(8,128)(2,1)S(1)}, u32[]{:S(2)}, u32[]{:S(2)}) collective-permute-start(bf16[512,3,128]{0,2,1:T(8,128)(2,1)S(1)} %fusion.16), channel_id=1, source_target_pairs={{8,0},{16,8},{24,16},{32,24},{40,32},{48,40},{56,48},{64,56},{72,6... | collective-permute-start | bytes 1179656 | tf_op jit(solution)/shard_map/ppermute | solution.py:13
  213.6 7.2 %collective-permute-start.2 = (bf16[512,3,128]{0,2,1:T(8,128)(2,1)S(1)}, bf16[512,3,128]{0,2,1:T(8,128)(2,1)S(1)}, u32[]{:S(2)}, u32[]{:S(2)}) collective-permute-start(bf16[512,3,128]{0,2,1:T(8,128)(2,1)S(1)} %fusion.15), channel_id=1, source_target_pairs={{8,0},{16,8},{24,16},{32,24},{40,32},{48,40},{56,48},{64,56},{72,6... | collective-permute-start | bytes 1179656 | tf_op jit(solution)/shard_map/ppermute | solution.py:13
  215.5 5.9 %slice-start = ((s8[7077888]{0:T(1024)(128)(4,1)}), s8[2883584]{0:T(1024)(128)(4,1)S(1)}, s32[]{:S(2)}) async-start(s8[7077888]{0:T(1024)(128)(4,1)} %bitcast.48), calls=%async_computation.4 | async-start | bytes 5767168
  217.1 4.3 %slice-start.1 = ((s8[7077888]{0:T(1024)(128)(4,1)}), s8[4194304]{0:T(1024)(128)(4,1)S(1)}, s32[]{:S(2)}) async-start(s8[7077888]{0:T(1024)(128)(4,1)} %bitcast.48), calls=%async_computation.5 | async-start | bytes 8388608
  227.3 110.5 %copy-start.2 = (bf16[64,3072]{1,0:T(8,128)(2,1)S(1)}, bf16[64,3072]{1,0:T(8,128)(2,1)}, u32[]{:S(2)}) copy-start(bf16[64,3072]{1,0:T(8,128)(2,1)} %param.5) | copy-start | bytes 1179652
  227.3 110.5 %copy-start.6 = (f32[3072]{0:T(1024)S(1)}, f32[3072]{0:T(1024)}, u32[]{:S(2)}) copy-start(f32[3072]{0:T(1024)} %param.7) | copy-start | bytes 36868
  227.3 111.8 %copy-start.3 = (bf16[64,3072]{1,0:T(8,128)(2,1)S(1)}, bf16[64,3072]{1,0:T(8,128)(2,1)}, u32[]{:S(2)}) copy-start(bf16[64,3072]{1,0:T(8,128)(2,1)} %param.6) | copy-start | bytes 1179652
Sparse Core Ops, SparseCore 0:
  10.0 94.6 all-gather.2
  107.3 88.1 all-gather.4
  227.4 110.3 reduce-scatter.1
where the time goes:
time: 348 us
  waiting for transfers between devices  272 us (78%)
  matrix products  29.5 us (8%)
  local copies, waits for them, and re-layouts  14.6 us (4%)
  between operations  13.4 us (4%)
  other arithmetic  9.71 us (3%)
  starting transfers between devices  8.65 us (2%)
    reduce_scatter x1, waiting for transfers between devices, shards(): lax.psum_scatter(lax.dot_general(grad_qkv, flat_w, (((1,), (1,)), ((), ()...  110 us
    all_gather x1, waiting for transfers between devices, shards(): lax.all_gather(hidden, 'head', axis=0, tiled=True)  83.8 us
    all_gather x1, waiting for transfers between devices, shards(): lax.all_gather(cotangent, 'head', axis=0, tiled=True)  73.9 us
    unnamed x19, local copies, waits for them, and re-layouts  10.3 us
    ppermute x4, starting transfers between devices, from_behind(): return lax.ppermute(block, axis, route)  8.57 us
    dot_general x1, matrix products, shards(): jnp.dot(lax.all_gather(hidden, 'head', axis=0, tiled=True), flat_w, prefe...  8.22 us
  transfers between devices with their start and end apart: 7, of which 4 were waited for; matrix products, arithmetic and copies ran while one was open for 12% of the time, Pallas kernels for 0%

commit v1 on v0

--- a/solution.py
+++ b/solution.py
@@ -30,7 +30,9 @@
     hidden = (normed * norm_gain).astype(jnp.bfloat16)
     flat_w = w_qkv.reshape(feature_count, 3 * local_width)
     projected = jnp.dot(
-        lax.all_gather(hidden, "head", axis=0, tiled=True),
+        jnp.concatenate(
+            lax.all_to_all(jnp.stack([hidden] * lax.axis_size("head")), "head", 0, 0), axis=0
+        ),
         flat_w,
         preferred_element_type=jnp.float32,
     ).astype(jnp.bfloat16)

time: 348 us -> 317 us (0.911)
  waiting for transfers between devices: 272 us -> 222 us
  starting transfers between devices: 8.65 us -> 24.1 us
    all_gather x1 -> x0, waiting for transfers between devices: 83.8 us -> none  [shards(): lax.all_gather(hidden, 'head', axis=0, tiled=True)]
    all_to_all x0 -> x1, waiting for transfers between devices: none -> 70.6 us  [shards(): lax.all_to_all(jnp.stack([hidden] * lax.axis_size('head')), 'head', 0, 0)]
    all_gather x1, waiting for transfers between devices: 73.9 us -> 36 us  [shards(): lax.all_gather(cotangent, 'head', axis=0, tiled=True)]
    all_to_all x0 -> x1, starting transfers between devices: none -> 10.9 us  [shards(): lax.all_to_all(jnp.stack([hidden] * lax.axis_size('head')), 'head', 0, 0)]
    ppermute x4, starting transfers between devices: 8.57 us -> 13.1 us  [from_behind(): return lax.ppermute(block, axis, route)]
  transfers between devices with their start and end apart: 7 -> 7, of which waited for: 4 -> 4; matrix products, arithmetic and copies ran while one was open for 12% -> 13% of each run, Pallas kernels for 0% -> 0%
where the time goes in v1:
time: 317 us; the launch traced here: 316 us
  waiting for transfers between devices  222 us (70%)
  matrix products  30 us (9%)
  starting transfers between devices  24.1 us (8%)
  local copies, waits for them, and re-layouts  16.6 us (5%)
  between operations  13.7 us (4%)
  other arithmetic  8.96 us (3%)
    reduce_scatter x1, waiting for transfers between devices, shards(): lax.psum_scatter(lax.dot_general(grad_qkv, flat_w, (((1,), (1,)), ((), ()...  112 us
    all_to_all x1, waiting for transfers between devices, shards(): lax.all_to_all(jnp.stack([hidden] * lax.axis_size('head')), 'head', 0, 0)  70.6 us
    all_gather x1, waiting for transfers between devices, shards(): lax.all_gather(cotangent, 'head', axis=0, tiled=True)  36 us
    ppermute x4, starting transfers between devices, from_behind(): return lax.ppermute(block, axis, route)  13.1 us
    all_to_all x1, starting transfers between devices, shards(): lax.all_to_all(jnp.stack([hidden] * lax.axis_size('head')), 'head', 0, 0)  10.9 us
    unnamed x19, local copies, waits for them, and re-layouts  10.3 us
    dot_general x1, matrix products, shards(): jnp.dot(jnp.concatenate(lax.all_to_all(jnp.stack([hidden] * lax.axis_size...  8.62 us
  transfers between devices with their start and end apart: 7, of which 4 were waited for; matrix products, arithmetic and copies ran while one was open for 13% of the time, Pallas kernels for 0%

profile of v1, /device:TPU:8, one launch (start us, length us, event | category | flops | bytes accessed | tf_op | source)
XLA Modules:
  0.0 315.9 jit_solution(13763728435365207676)
XLA Ops:
  6.5 0.0 copy-start
  6.5 1.3 fusion.33
  7.9 1.2 fusion.27
  9.0 2.0 stack.2
  11.1 10.9 %all-to-all-start = ((bf16[8,64,3072]{2,1,0:T(8,128)(2,1)}), bf16[8,64,3072]{2,1,0:T(8,128)(2,1)}, u32[]{:S(2)}, u32[]{:S(2)}) async-start(bf16[8,64,3072]{2,1,0:T(8,128)(2,1)} %stack.2), calls=%async_computation | async-start | bytes 6291456 | tf_op jit(solution)/shard_map/all_to_all | solution.py:34
  22.0 0.0 all-gather.2.cloned.1.call-start
  22.0 0.7 all-gather.2.cloned.1.call-update
  22.7 0.0 reduce-scatter.2.cloned.1.call-start
  22.8 10.3 %copy.24 = bf16[3072,3,384]{0,2,1:T(8,128)(2,1)} copy(bf16[3072,3,384]{2,0,1:T(8,128)(2,1)} %param.8) | data formatting | bytes 14155776 | tf_op args[3]
  33.0 70.6 %all-to-all-done = bf16[8,64,3072]{2,1,0:T(8,128)(2,1)} async-done(((bf16[8,64,3072]{2,1,0:T(8,128)(2,1)}), bf16[8,64,3072]{2,1,0:T(8,128)(2,1)}, u32[]{:S(2)}, u32[]{:S(2)}) %all-to-all-start) | async-done | bytes 3145760 | tf_op jit(solution)/shard_map/all_to_all | solution.py:34
  103.7 8.6 %convolution_convert_fusion.1 = bf16[512,1152]{1,0:T(8,128)(2,1)S(1)} fusion(bf16[512,3072]{1,0:T(8,128)(2,1)} %bitcast, bf16[3072,1152]{0,1:T(8,128)(2,1)} %bitcast.48), kind=kOutput, calls=%fused_computation.7 | convolution fusion | flops 3624468480 | bytes 11403264 | tf_op jit(solution)/shard_map/dot_general | solution.py:32
  112.3 0.9 fusion.39
  113.2 0.2 copy.31
  113.4 0.9 copy.34
  114.3 1.2 copy.25
  115.5 0.9 copy.29
  116.4 1.9 collective-permute-start
  118.3 3.1 collective-permute-start.1
  121.4 36.0 %all-gather.2.cloned.1.call-done = bf16[512,3072]{1,0:T(8,128)(2,1)} async-done(((bf16[64,3072]{1,0:T(8,128)(2,1)}), bf16[512,3072]{1,0:T(8,128)(2,1)}) %all-gather.2.cloned.1.call-update) | async-done | bytes 3145744 | tf_op jit(solution)/shard_map/all_gather | solution.py:48
  157.4 0.0 copy-done
  157.4 3.3 %convolution_convert_fusion.3 = bf16[512,384]{0,1:T(8,128)(2,1)S(1)} fusion(bf16[512,3072]{1,0:T(8,128)(2,1)} %all-gather.2.cloned.1.call-done, bf16[384,3072]{1,0:T(8,128)(2,1)S(1)} %copy-done), kind=kOutput, calls=%fused_computation.23 | convolution fusion | flops 1208156160 | bytes 5898240 | tf_op jit(solution)/shard_map/dot_general | solution.py:47
  160.7 0.0 copy-start.4
  160.7 2.3 fusion.40
  163.1 0.0 copy-done.4
  163.1 0.2 copy.26
  163.3 0.6 multiply_reduce_fusion.3
  163.9 0.0 collective-permute-done
  163.9 1.6 multiply_reduce_fusion.2
  165.5 0.0 copy-start.5
  165.5 1.1 fusion.3
  166.7 0.0 copy-done.5
  166.7 0.0 copy-start.1
  166.7 0.9 fusion.16
  167.6 5.3 %collective-permute-start.3 = (bf16[512,3,128]{0,2,1:T(8,128)(2,1)S(1)}, bf16[512,3,128]{0,2,1:T(8,128)(2,1)S(1)}, u32[]{:S(2)}, u32[]{:S(2)}) collective-permute-start(bf16[512,3,128]{0,2,1:T(8,128)(2,1)S(1)} %fusion.16), channel_id=1, source_target_pairs={{8,0},{16,8},{24,16},{32,24},{40,32},{48,40},{56,48},{64,56},{72,6... | collective-permute-start | bytes 1179656 | tf_op jit(solution)/shard_map/ppermute | solution.py:13
  173.0 0.0 collective-permute-done.1
  173.0 0.0 copy-done.1
  173.0 2.7 multiply_reduce_fusion
  175.7 2.0 multiply_convert_fusion
  177.7 0.4 fusion.41
  178.1 0.6 fusion.15
  178.7 2.8 collective-permute-start.2
  181.5 0.0 slice-start
  181.6 1.6 fusion.14
  183.1 0.0 slice-start.1
  183.1 0.0 collective-permute-done.3
  183.1 0.9 add_convert_fusion
  184.0 2.8 collective-permute-done.2
  186.8 0.6 add_convert_fusion.1
  187.5 0.0 slice-done
  187.5 0.0 slice-done.1
  187.5 5.8 %convolution_convert_fusion = bf16[512,3072]{1,0:T(8,128)(2,1)} fusion(bf16[3072,1152]{0,1:T(8,128)(2,1)S(1)} %bitcast.51, bf16[512,384]{0,1:T(8,128)(2,1)S(1)} %bitcast.63, bf16[512,384]{0,1:T(8,128)(2,1)S(1)} %bitcast.58, bf16[512,384]{0,1:T(8,128)(2,1)S(1)} %bitcast.57), kind=kOutput, calls=%fused_computation | convolution fusion | flops 3628990464 | bytes 11403264 | tf_op jit(solution)/shard_map/dot_general | solution.py:97
  193.3 0.0 copy-start.2
  193.3 0.0 copy-start.6
  193.3 0.0 copy-start.3
  193.3 0.0 reduce-scatter.2.cloned.1.call-update
  193.4 112.3 %reduce-scatter.2.cloned.1.call-done = bf16[64,3072]{1,0:T(8,128)(2,1)} async-done(((bf16[512,3072]{1,0:T(8,128)(2,1)}), bf16[64,3072]{1,0:T(8,128)(2,1)}) %reduce-scatter.2.cloned.1.call-update) | async-done | bytes 393232 | tf_op jit(solution)/shard_map/reduce_scatter | solution.py:96
  305.7 0.0 copy-done.2
  305.7 0.0 copy-done.6
  305.7 1.3 fusion.28
  307.0 0.0 copy-done.3
  307.0 2.0 fusion.32
  (6 shorter events, 0.0 us)
Async XLA Ops:
  6.5 150.9 %copy-start = (bf16[384,3072]{1,0:T(8,128)(2,1)S(1)}, bf16[384,3072]{1,0:T(8,128)(2,1)}, u32[]{:S(2)}) copy-start(bf16[384,3072]{1,0:T(8,128)(2,1)} %param.9) | copy-start | bytes 7077892
  11.1 92.6 %all-to-all-start = ((bf16[8,64,3072]{2,1,0:T(8,128)(2,1)}), bf16[8,64,3072]{2,1,0:T(8,128)(2,1)}, u32[]{:S(2)}, u32[]{:S(2)}) async-start(bf16[8,64,3072]{2,1,0:T(8,128)(2,1)} %stack.2), calls=%async_computation | async-start | bytes 6291456 | tf_op jit(solution)/shard_map/all_to_all | solution.py:34
  22.0 135.4 %all-gather.2.cloned.1.call-start = ((), (), s32[]{:S(2)}) async-start(), calls=%async_computation.2 | async-start | bytes 3538944 | tf_op jit(solution)/shard_map/all_gather | solution.py:48
  22.7 283.0 %reduce-scatter.2.cloned.1.call-start = ((), (), s32[]{:S(2)}) async-start(), calls=%async_computation.3 | async-start | bytes 3538944 | tf_op jit(solution)/shard_map/reduce_scatter | solution.py:96
  116.4 47.5 %collective-permute-start = (bf16[512,3,128]{2,0,1:T(8,128)(2,1)}, bf16[512,3,128]{2,0,1:T(8,128)(2,1)}, u32[]{:S(2)}, u32[]{:S(2)}) collective-permute-start(bf16[512,3,128]{2,0,1:T(8,128)(2,1)} %copy.29), channel_id=1, source_target_pairs={{0,8},{8,16},{16,24},{24,32},{32,40},{40,48},{48,56},{56,64},{64,7... | collective-permute-start | bytes 1179656 | tf_op jit(solution)/shard_map/ppermute | solution.py:13
  118.3 54.6 %collective-permute-start.1 = (bf16[512,3,128]{2,0,1:T(8,128)(2,1)}, bf16[512,3,128]{2,0,1:T(8,128)(2,1)}, u32[]{:S(2)}, u32[]{:S(2)}) collective-permute-start(bf16[512,3,128]{2,0,1:T(8,128)(2,1)} %copy.34), channel_id=1, source_target_pairs={{0,8},{8,16},{16,24},{24,32},{32,40},{40,48},{48,56},{56,64},{64,7... | collective-permute-start | bytes 1179656 | tf_op jit(solution)/shard_map/ppermute | solution.py:13
  160.7 2.4 copy-start.4
  165.5 1.2 copy-start.5
  166.7 6.3 %copy-start.1 = (f32[3,512,512]{1,2,0:T(8,128)S(1)}, f32[3,512,512]{1,2,0:T(8,128)}, u32[]{:S(2)}) copy-start(f32[3,512,512]{1,2,0:T(8,128)} %fusion.40) | copy-start | bytes 9437188
  167.6 15.5 %collective-permute-start.3 = (bf16[512,3,128]{0,2,1:T(8,128)(2,1)S(1)}, bf16[512,3,128]{0,2,1:T(8,128)(2,1)S(1)}, u32[]{:S(2)}, u32[]{:S(2)}) collective-permute-start(bf16[512,3,128]{0,2,1:T(8,128)(2,1)S(1)} %fusion.16), channel_id=1, source_target_pairs={{8,0},{16,8},{24,16},{32,24},{40,32},{48,40},{56,48},{64,56},{72,6... | collective-permute-start | bytes 1179656 | tf_op jit(solution)/shard_map/ppermute | solution.py:13
  178.7 8.1 %collective-permute-start.2 = (bf16[512,3,128]{0,2,1:T(8,128)(2,1)S(1)}, bf16[512,3,128]{0,2,1:T(8,128)(2,1)S(1)}, u32[]{:S(2)}, u32[]{:S(2)}) collective-permute-start(bf16[512,3,128]{0,2,1:T(8,128)(2,1)S(1)} %fusion.15), channel_id=1, source_target_pairs={{8,0},{16,8},{24,16},{32,24},{40,32},{48,40},{56,48},{64,56},{72,6... | collective-permute-start | bytes 1179656 | tf_op jit(solution)/shard_map/ppermute | solution.py:13
  181.5 5.9 %slice-start = ((s8[7077888]{0:T(1024)(128)(4,1)}), s8[2883584]{0:T(1024)(128)(4,1)S(1)}, s32[]{:S(2)}) async-start(s8[7077888]{0:T(1024)(128)(4,1)} %bitcast.49), calls=%async_computation.4 | async-start | bytes 5767168
  183.1 4.4 %slice-start.1 = ((s8[7077888]{0:T(1024)(128)(4,1)}), s8[4194304]{0:T(1024)(128)(4,1)S(1)}, s32[]{:S(2)}) async-start(s8[7077888]{0:T(1024)(128)(4,1)} %bitcast.49), calls=%async_computation.5 | async-start | bytes 8388608
  193.3 112.4 %copy-start.2 = (bf16[64,3072]{1,0:T(8,128)(2,1)S(1)}, bf16[64,3072]{1,0:T(8,128)(2,1)}, u32[]{:S(2)}) copy-start(bf16[64,3072]{1,0:T(8,128)(2,1)} %param.5) | copy-start | bytes 1179652
  193.3 112.4 %copy-start.6 = (f32[3072]{0:T(1024)S(1)}, f32[3072]{0:T(1024)}, u32[]{:S(2)}) copy-start(f32[3072]{0:T(1024)} %param.7) | copy-start | bytes 36868
  193.3 113.7 %copy-start.3 = (bf16[64,3072]{1,0:T(8,128)(2,1)S(1)}, bf16[64,3072]{1,0:T(8,128)(2,1)}, u32[]{:S(2)}) copy-start(bf16[64,3072]{1,0:T(8,128)(2,1)} %param.6) | copy-start | bytes 1179652
Sparse Core Ops, SparseCore 0:
  25.4 131.9 all-gather.1
  193.5 112.1 reduce-scatter.1
